TPU v7x, 128 devices: a whole 4x4x4 slice. The times are simulated.
128 devices in a mesh: pipe: 2 (over x_lo), seq: 32 (over z, y, x_hi), tp: 2 (over core).
Axes of the slice: x: 4 (x_hi: 2, x_lo: 2; x = x_hi * 2 + x_lo), y: 4, z: 4, core: 2. Of those that a mesh axis runs over, the one named last changes fastest.
Arguments:
- queries: bfloat16 [14336, 4096], P(('pipe', 'seq', 'tp')), may hold values from -45 to 45
- keys: bfloat16 [14336, 4096], P(('pipe', 'seq', 'tp')), may hold values from -8 to 8
- values: bfloat16 [14336, 4096], P(('pipe', 'seq', 'tp')), may hold values from -6 to 6
- stale_keys: bfloat16 [14336, 4096], P(('pipe', 'seq', 'tp')), may hold values from -8 to 8
- stale_values: bfloat16 [14336, 4096], P(('pipe', 'seq', 'tp')), may hold values from -6 to 6
- group_order: int32 [2, 4], replicated, may hold values from 0 to 3, each once within a row
Outputs:
- attended: bfloat16 [14336, 4096], P(('pipe', 'seq', 'tp'))
All inputs are finite; a program needn't handle non-finite values.
Results may differ from a plain program's by a relative error of at most 0.025.
Values may be sent and summed in bfloat16 or wider, within the bound.
A program may use at most 128 MiB of HBM per device.

v0:
```python
import math

import jax
import jax.numpy as jnp
from jax import lax
from jax.sharding import PartitionSpec as P

GPS = 4


def group_times(group_order):
    sections, groups = group_order.shape
    match = group_order[:, :, None] == jnp.arange(groups, dtype=jnp.int32)[None, None, :]
    turns = jnp.sum(
        jnp.arange(groups, dtype=jnp.int32)[None, :, None] * match.astype(jnp.int32), axis=1
    )
    return (turns + jnp.arange(sections, dtype=jnp.int32)[:, None]).reshape(sections * groups)


def table_lookup(table, position):
    match = position[:, None] == jnp.arange(table.shape[0], dtype=jnp.int32)[None, :]
    return jnp.sum(jnp.where(match, table[None, :], 0), axis=1)


def key_block_size(count_rows):
    size_block = count_rows
    while size_block > 2048 and size_block % 2 == 0:
        size_block = size_block // 2
    return size_block


def attend(carry, query_blocks, query_groups, query_times, piece, local_rows, tp_count, timing):
    fresh_keys, fresh_values, old_keys, old_values = piece
    count_rows = fresh_keys.shape[0]
    size_block = key_block_size(count_rows)
    head_size = fresh_keys.shape[1]
    per_group = local_rows // GPS
    scaling = 1.0 / math.sqrt(head_size)
    block_count = query_blocks.shape[0]

    def step_block(block_index, state):
        peaks, totals, sums = state
        offset = block_index * size_block
        part_keys = lax.dynamic_slice_in_dim(fresh_keys, offset, size_block, 0)
        part_values = lax.dynamic_slice_in_dim(fresh_values, offset, size_block, 0)
        part_old_keys = lax.dynamic_slice_in_dim(old_keys, offset, size_block, 0)
        part_old_values = lax.dynamic_slice_in_dim(old_values, offset, size_block, 0)
        global_row = offset + jnp.arange(size_block, dtype=jnp.int32)
        device_row = global_row // local_rows
        key_section = device_row // tp_count
        within = global_row % local_rows
        key_group = key_section * GPS + within // per_group
        key_time = table_lookup(timing, key_group)
        new_peaks = []
        new_totals = []
        new_sums = []
        for number in range(block_count):
            fresh = (key_time < query_times[number]) | (key_group == query_groups[number])
            chosen_keys = jnp.where(fresh[:, None], part_keys, part_old_keys)
            chosen_values = jnp.where(fresh[:, None], part_values, part_old_values)
            scores = (
                lax.dot_general(
                    query_blocks[number],
                    chosen_keys,
                    (((1,), (1,)), ((), ())),
                    preferred_element_type=jnp.float32,
                )
                * scaling
            )
            peak_new = jnp.maximum(peaks[number], jnp.max(scores, axis=1))
            factor = jnp.exp(peaks[number] - peak_new)
            weights = jnp.exp(scores - peak_new[:, None])
            new_totals.append(totals[number] * factor + jnp.sum(weights, axis=1))
            product = jnp.dot(
                weights.astype(jnp.bfloat16), chosen_values, preferred_element_type=jnp.float32
            )
            new_sums.append(sums[number] * factor[:, None] + product)
            new_peaks.append(peak_new)
        return (jnp.stack(new_peaks), jnp.stack(new_totals), jnp.stack(new_sums))

    return lax.fori_loop(0, count_rows // size_block, step_block, carry)


def starting_state(block_count, per_group, head_size):
    return (
        jnp.full((block_count, per_group), -1e30, jnp.float32),
        jnp.zeros((block_count, per_group), jnp.float32),
        jnp.zeros((block_count, per_group, head_size), jnp.float32),
    )


def local(queries, keys, values, stale_keys, stale_values, group_order):
    tp_count = lax.axis_size("tp")
    section = lax.axis_index("pipe")
    moved = (
        lax.all_to_all(queries, "seq", split_axis=1, concat_axis=0, tiled=True),
        lax.all_to_all(keys, "seq", split_axis=1, concat_axis=0, tiled=True),
        lax.all_to_all(values, "seq", split_axis=1, concat_axis=0, tiled=True),
        lax.all_to_all(stale_keys, "seq", split_axis=1, concat_axis=0, tiled=True),
        lax.all_to_all(stale_values, "seq", split_axis=1, concat_axis=0, tiled=True),
    )
    head_queries, fresh_keys, fresh_values, old_keys, old_values = moved
    local_rows = head_queries.shape[0]
    head_size = head_queries.shape[1]
    per_group = local_rows // GPS
    timing = group_times(group_order)
    own_groups = section * GPS + jnp.arange(GPS, dtype=jnp.int32)
    own_times = table_lookup(timing, own_groups)
    own_blocks = head_queries.reshape(GPS, per_group, head_size)
    peaks, totals, sums = attend(
        starting_state(GPS, per_group, head_size),
        own_blocks,
        own_groups,
        own_times,
        (
            lax.all_gather(fresh_keys, ("pipe", "tp"), axis=0, tiled=True),
            lax.all_gather(fresh_values, ("pipe", "tp"), axis=0, tiled=True),
            lax.all_gather(old_keys, ("pipe", "tp"), axis=0, tiled=True),
            lax.all_gather(old_values, ("pipe", "tp"), axis=0, tiled=True),
        ),
        local_rows,
        tp_count,
        timing,
    )
    mixed = (sums / totals[..., None]).astype(jnp.bfloat16).reshape(local_rows, head_size)
    return lax.all_to_all(mixed, "seq", split_axis=0, concat_axis=1, tiled=True)


def solution(mesh):
    in_specs = (
        P(("pipe", "seq", "tp"), None),
        P(("pipe", "seq", "tp"), None),
        P(("pipe", "seq", "tp"), None),
        P(("pipe", "seq", "tp"), None),
        P(("pipe", "seq", "tp"), None),
        P(),
    )
    out_specs = P(("pipe", "seq", "tp"), None)
    return jax.shard_map(local, mesh=mesh, in_specs=in_specs, out_specs=out_specs, check_vma=False)
```

profile of v0, /device:TPU:96, one launch (start us, length us, event | category | flops | bytes accessed | tf_op | source)
XLA Modules:
  0.0 514.8 jit_solution(6606538611814151689)
XLA Ops:
  7.9 25.5 %all_to_all.111 = bf16[112,32,128]{2,0,1:T(8,128)(2,1)} all-to-all(bf16[112,32,128]{2,0,1:T(8,128)(2,1)S(1)} %copy_bitcast_fusion.5), channel_id=1, replica_groups=mesh['pipe'=2,'seq'=32,'tp'=2] {'seq'}, dimensions={1} | all-to-all | bytes 1835008 | tf_op jit(solution)/shard_map/all_to_all | solution.py:97
  34.8 30.0 %all_to_all.112 = bf16[112,32,128]{2,0,1:T(8,128)(2,1)} all-to-all(bf16[112,32,128]{2,0,1:T(8,128)(2,1)S(1)} %copy_bitcast_fusion.2), channel_id=1, replica_groups=mesh['pipe'=2,'seq'=32,'tp'=2] {'seq'}, dimensions={1} | all-to-all | bytes 1835008 | tf_op jit(solution)/shard_map/all_to_all | solution.py:98
  65.1 29.6 %all_to_all.113 = bf16[112,32,128]{2,0,1:T(8,128)(2,1)} all-to-all(bf16[112,32,128]{2,0,1:T(8,128)(2,1)S(1)} %copy_bitcast_fusion.4), channel_id=1, replica_groups=mesh['pipe'=2,'seq'=32,'tp'=2] {'seq'}, dimensions={1} | all-to-all | bytes 1835008 | tf_op jit(solution)/shard_map/all_to_all | solution.py:99
  95.0 25.6 %all_to_all.114 = bf16[112,32,128]{2,0,1:T(8,128)(2,1)} all-to-all(bf16[112,32,128]{2,0,1:T(8,128)(2,1)S(1)} %copy_bitcast_fusion.1), channel_id=1, replica_groups=mesh['pipe'=2,'seq'=32,'tp'=2] {'seq'}, dimensions={1} | all-to-all | bytes 1835008 | tf_op jit(solution)/shard_map/all_to_all | solution.py:100
  121.7 6.1 %all-to-all-start.2 = ((bf16[112,32,128]{2,0,1:T(8,128)(2,1)}), bf16[112,32,128]{2,0,1:T(8,128)(2,1)S(1)}, u32[]{:S(2)}, u32[]{:S(2)}) async-start(bf16[112,32,128]{2,0,1:T(8,128)(2,1)} %copy_bitcast_fusion.3), calls=%async_computation.2 | async-start | bytes 1835008 | tf_op jit(solution)/shard_map/all_to_all | solution.py:96
  128.2 21.5 %all-to-all-done.2 = bf16[112,32,128]{2,0,1:T(8,128)(2,1)S(1)} async-done(((bf16[112,32,128]{2,0,1:T(8,128)(2,1)}), bf16[112,32,128]{2,0,1:T(8,128)(2,1)S(1)}, u32[]{:S(2)}, u32[]{:S(2)}) %all-to-all-start.2) | async-done | bytes 917536 | tf_op jit(solution)/shard_map/all_to_all | solution.py:96
  149.8 42.9 %all-gather.7.cloned.1.call-done = bf16[14336,128]{1,0:T(8,128)(2,1)} async-done(((bf16[3584,128]{1,0:T(8,128)(2,1)}), bf16[14336,128]{1,0:T(8,128)(2,1)}) %all-gather.7.cloned.1.call-update) | async-done | bytes 3670032 | tf_op jit(solution)/shard_map/all_gather | solution.py:118
  192.7 44.6 %all-gather.11.cloned.1.call-done = bf16[14336,128]{1,0:T(8,128)(2,1)} async-done(((bf16[3584,128]{1,0:T(8,128)(2,1)}), bf16[14336,128]{1,0:T(8,128)(2,1)}) %all-gather.11.cloned.1.call-update) | async-done | bytes 3670032 | tf_op jit(solution)/shard_map/all_gather | solution.py:119
  237.4 243.4 %while.21 = (s32[]{:T(128)}, f32[4,896]{1,0:T(4,128)S(1)}, f32[4,896]{1,0:T(4,128)S(1)}, f32[4,896,128]{2,1,0:T(8,128)S(1)}, s32[2,4]{1,0:T(2,128)}, /*index=5*/...) while((s32[]{:T(128)}, f32[4,896]{1,0:T(4,128)S(1)}, ...), condition=%wide.wide.region_12.13_spmd, body=%wide.wide.region_2.12_spmd.sunk | while | flops 3344078080 | bytes 126055616 | solution.py:81
  238.4 5.3 %compare_or_fusion.6 = (pred[1792]{0:T(1024)(128)(4,1)S(1)}, pred[1792]{0:T(1024)(128)(4,1)S(1)}, pred[1792]{0:T(1024)(128)(4,1)S(1)}, pred[1792]{0:T(1024)(128)(4,1)S(1)}) fusion(s32[1792]{0:T(1024)S(1)} %select_reduce_fusion.5, s32[]{:T(128)} %bitcast.151, s32[]{:T(128)} %bitcast.152, s32[]{:T(128)S(6)} %mul.440, s32[]{:T(128)} %bitcast.153, ...), kind=kLoop, calls=%fused_computation.114.clone.clone.1 | loop fusion | flops 89600 | bytes 14372 | tf_op jit(solution)/shard_map/while/body/eval_jaxpr/or | solution.py:58
  243.8 3.2 multiply_reduce_fusion.12
  268.8 5.3 %compare_or_fusion.6 = (pred[1792]{0:T(1024)(128)(4,1)S(1)}, pred[1792]{0:T(1024)(128)(4,1)S(1)}, pred[1792]{0:T(1024)(128)(4,1)S(1)}, pred[1792]{0:T(1024)(128)(4,1)S(1)}) fusion(s32[1792]{0:T(1024)S(1)} %select_reduce_fusion.5, s32[]{:T(128)} %bitcast.151, s32[]{:T(128)} %bitcast.152, s32[]{:T(128)S(6)} %mul.440, s32[]{:T(128)} %bitcast.153, ...), kind=kLoop, calls=%fused_computation.114.clone.clone.1 | loop fusion | flops 89600 | bytes 14372 | tf_op jit(solution)/shard_map/while/body/eval_jaxpr/or | solution.py:58
  274.2 3.2 multiply_reduce_fusion.12
  299.2 5.3 %compare_or_fusion.6 = (pred[1792]{0:T(1024)(128)(4,1)S(1)}, pred[1792]{0:T(1024)(128)(4,1)S(1)}, pred[1792]{0:T(1024)(128)(4,1)S(1)}, pred[1792]{0:T(1024)(128)(4,1)S(1)}) fusion(s32[1792]{0:T(1024)S(1)} %select_reduce_fusion.5, s32[]{:T(128)} %bitcast.151, s32[]{:T(128)} %bitcast.152, s32[]{:T(128)S(6)} %mul.440, s32[]{:T(128)} %bitcast.153, ...), kind=kLoop, calls=%fused_computation.114.clone.clone.1 | loop fusion | flops 89600 | bytes 14372 | tf_op jit(solution)/shard_map/while/body/eval_jaxpr/or | solution.py:58
  304.6 3.2 multiply_reduce_fusion.12
  329.6 5.3 %compare_or_fusion.6 = (pred[1792]{0:T(1024)(128)(4,1)S(1)}, pred[1792]{0:T(1024)(128)(4,1)S(1)}, pred[1792]{0:T(1024)(128)(4,1)S(1)}, pred[1792]{0:T(1024)(128)(4,1)S(1)}) fusion(s32[1792]{0:T(1024)S(1)} %select_reduce_fusion.5, s32[]{:T(128)} %bitcast.151, s32[]{:T(128)} %bitcast.152, s32[]{:T(128)S(6)} %mul.440, s32[]{:T(128)} %bitcast.153, ...), kind=kLoop, calls=%fused_computation.114.clone.clone.1 | loop fusion | flops 89600 | bytes 14372 | tf_op jit(solution)/shard_map/while/body/eval_jaxpr/or | solution.py:58
  335.0 3.2 multiply_reduce_fusion.12
  360.0 5.3 %compare_or_fusion.6 = (pred[1792]{0:T(1024)(128)(4,1)S(1)}, pred[1792]{0:T(1024)(128)(4,1)S(1)}, pred[1792]{0:T(1024)(128)(4,1)S(1)}, pred[1792]{0:T(1024)(128)(4,1)S(1)}) fusion(s32[1792]{0:T(1024)S(1)} %select_reduce_fusion.5, s32[]{:T(128)} %bitcast.151, s32[]{:T(128)} %bitcast.152, s32[]{:T(128)S(6)} %mul.440, s32[]{:T(128)} %bitcast.153, ...), kind=kLoop, calls=%fused_computation.114.clone.clone.1 | loop fusion | flops 89600 | bytes 14372 | tf_op jit(solution)/shard_map/while/body/eval_jaxpr/or | solution.py:58
  365.4 3.2 multiply_reduce_fusion.12
  390.4 5.3 %compare_or_fusion.6 = (pred[1792]{0:T(1024)(128)(4,1)S(1)}, pred[1792]{0:T(1024)(128)(4,1)S(1)}, pred[1792]{0:T(1024)(128)(4,1)S(1)}, pred[1792]{0:T(1024)(128)(4,1)S(1)}) fusion(s32[1792]{0:T(1024)S(1)} %select_reduce_fusion.5, s32[]{:T(128)} %bitcast.151, s32[]{:T(128)} %bitcast.152, s32[]{:T(128)S(6)} %mul.440, s32[]{:T(128)} %bitcast.153, ...), kind=kLoop, calls=%fused_computation.114.clone.clone.1 | loop fusion | flops 89600 | bytes 14372 | tf_op jit(solution)/shard_map/while/body/eval_jaxpr/or | solution.py:58
  395.8 3.2 multiply_reduce_fusion.12
  420.8 5.3 %compare_or_fusion.6 = (pred[1792]{0:T(1024)(128)(4,1)S(1)}, pred[1792]{0:T(1024)(128)(4,1)S(1)}, pred[1792]{0:T(1024)(128)(4,1)S(1)}, pred[1792]{0:T(1024)(128)(4,1)S(1)}) fusion(s32[1792]{0:T(1024)S(1)} %select_reduce_fusion.5, s32[]{:T(128)} %bitcast.151, s32[]{:T(128)} %bitcast.152, s32[]{:T(128)S(6)} %mul.440, s32[]{:T(128)} %bitcast.153, ...), kind=kLoop, calls=%fused_computation.114.clone.clone.1 | loop fusion | flops 89600 | bytes 14372 | tf_op jit(solution)/shard_map/while/body/eval_jaxpr/or | solution.py:58
  451.2 5.3 %compare_or_fusion.6 = (pred[1792]{0:T(1024)(128)(4,1)S(1)}, pred[1792]{0:T(1024)(128)(4,1)S(1)}, pred[1792]{0:T(1024)(128)(4,1)S(1)}, pred[1792]{0:T(1024)(128)(4,1)S(1)}) fusion(s32[1792]{0:T(1024)S(1)} %select_reduce_fusion.5, s32[]{:T(128)} %bitcast.151, s32[]{:T(128)} %bitcast.152, s32[]{:T(128)S(6)} %mul.440, s32[]{:T(128)} %bitcast.153, ...), kind=kLoop, calls=%fused_computation.114.clone.clone.1 | loop fusion | flops 89600 | bytes 14372 | tf_op jit(solution)/shard_map/while/body/eval_jaxpr/or | solution.py:58
  481.4 25.9 %all_to_all.115 = bf16[32,112,128]{2,1,0:T(8,128)(2,1)S(1)} all-to-all(bf16[32,112,128]{2,1,0:T(8,128)(2,1)S(1)} %bitcast.164), channel_id=1, replica_groups=mesh['pipe'=2,'seq'=32,'tp'=2] {'seq'}, dimensions={0} | all-to-all | bytes 1835008 | tf_op jit(solution)/shard_map/all_to_all | solution.py:126
  (274 shorter events, 186.9 us)
Async XLA Ops:
  6.5 58.4 %copy-start.5 = (bf16[112,4096]{1,0:T(8,128)(2,1)S(1)}, bf16[112,4096]{1,0:T(8,128)(2,1)}, u32[]{:S(2)}) copy-start(bf16[112,4096]{1,0:T(8,128)(2,1)} %param.11) | copy-start | bytes 2752516
  6.5 143.2 %all-gather.5.cloned.1.call-start = ((), (), s32[]{:S(2)}) async-start(), calls=%async_computation.6 | async-start | bytes 4587520 | tf_op jit(solution)/shard_map/all_gather | solution.py:116
  7.9 86.9 %copy-start.6 = (bf16[112,4096]{1,0:T(8,128)(2,1)S(1)}, bf16[112,4096]{1,0:T(8,128)(2,1)}, u32[]{:S(2)}) copy-start(bf16[112,4096]{1,0:T(8,128)(2,1)} %param.12) | copy-start | bytes 2752516
  33.4 116.3 %all-gather.9.cloned.1.call-start = ((), (), s32[]{:S(2)}) async-start(), calls=%async_computation.8 | async-start | bytes 4587520 | tf_op jit(solution)/shard_map/all_gather | solution.py:117
  64.9 62.9 %copy-start.8 = (s32[2,4]{1,0:T(2,128)S(1)}, s32[2,4]{1,0:T(2,128)}, u32[]{:S(2)}) copy-start(s32[2,4]{1,0:T(2,128)} %param.13) | copy-start | bytes 100
  64.9 127.8 %all-gather.7.cloned.1.call-start = ((), (), s32[]{:S(2)}) async-start(), calls=%async_computation.7 | async-start | bytes 4587520 | tf_op jit(solution)/shard_map/all_gather | solution.py:118
  65.1 55.5 %copy-start.7 = (bf16[112,4096]{1,0:T(8,128)(2,1)S(1)}, bf16[112,4096]{1,0:T(8,128)(2,1)}, u32[]{:S(2)}) copy-start(bf16[112,4096]{1,0:T(8,128)(2,1)} %param.8) | copy-start | bytes 2752516
  94.7 142.5 %all-gather.11.cloned.1.call-start = ((), (), s32[]{:S(2)}) async-start(), calls=%async_computation.9 | async-start | bytes 4587520 | tf_op jit(solution)/shard_map/all_gather | solution.py:119
  121.7 28.1 %all-to-all-start.2 = ((bf16[112,32,128]{2,0,1:T(8,128)(2,1)}), bf16[112,32,128]{2,0,1:T(8,128)(2,1)S(1)}, u32[]{:S(2)}, u32[]{:S(2)}) async-start(bf16[112,32,128]{2,0,1:T(8,128)(2,1)} %copy_bitcast_fusion.3), calls=%async_computation.2 | async-start | bytes 1835008 | tf_op jit(solution)/shard_map/all_to_all | solution.py:96
  127.9 109.4 %copy-start.9 = (s32[2,4]{1,0:T(2,128)}, s32[2,4]{1,0:T(2,128)S(1)}, u32[]{:S(2)}) copy-start(s32[2,4]{1,0:T(2,128)S(1)} %iota_add_fusion.1) | copy-start | bytes 100
  149.7 87.5 %copy-start.1 = (bf16[112,32,128]{2,0,1:T(8,128)(2,1)}, bf16[112,32,128]{2,0,1:T(8,128)(2,1)S(1)}, u32[]{:S(2)}) copy-start(bf16[112,32,128]{2,0,1:T(8,128)(2,1)S(1)} %all-to-all-done.2) | copy-start | bytes 2752516
  243.8 4.3 copy-start.4
  247.0 2.0 copy-start.3
  274.2 4.3 copy-start.4
  277.4 2.0 copy-start.3
  304.6 4.3 copy-start.4
  307.8 2.0 copy-start.3
  335.0 4.3 copy-start.4
  338.2 2.0 copy-start.3
  365.4 4.3 copy-start.4
  368.6 2.0 copy-start.3
  395.8 4.3 copy-start.4
  426.2 4.3 copy-start.4
  456.6 4.3 copy-start.4
  (12 other events, 20.5 us)
Sparse Core Ops, SparseCore 0:
  33.6 55.5 all-gather.4
  90.8 56.5 all-gather.8
  149.1 43.5 all-gather.6
  194.2 43.0 all-gather.10
where the time goes:
time: 520 us; the launch traced here: 515 us
  matrix products  148 us (28%)
  blocking collectives  137 us (26%)
  waiting for transfers between devices  109 us (21%)
  other arithmetic  81.3 us (16%)
  local copies, waits for them, and re-layouts  18.5 us (4%)
  between operations  13.3 us (3%)
  starting transfers between devices  6.2 us (1%)
    dot_general x32, matrix products, step_block(): lax.dot_general(query_blocks[number], chosen_keys, (((1,), (1,)), ((), ()...  95.5 us
    dot_general x32, matrix products, step_block(): jnp.dot(weights.astype(jnp.bfloat16), chosen_values, preferred_element_ty...  52.6 us
    all_gather x1, waiting for transfers between devices, local(): lax.all_gather(old_values, ('pipe', 'tp'), axis=0, tiled=True)  44.6 us
    all_gather x1, waiting for transfers between devices, local(): lax.all_gather(old_keys, ('pipe', 'tp'), axis=0, tiled=True)  42.9 us
    or x8, other arithmetic, step_block(): (key_time < query_times[number]) | (key_group == query_groups[number])  42.2 us
    reduce_sum x32, other arithmetic, step_block(): new_totals.append(totals[number] * factor + jnp.sum(weights, axis=1))  35.4 us
    all_to_all x1, blocking collectives, local(): lax.all_to_all(values, 'seq', split_axis=1, concat_axis=0, tiled=True)  30 us
    all_to_all x1, blocking collectives, local(): lax.all_to_all(stale_keys, 'seq', split_axis=1, concat_axis=0, tiled=True)  29.6 us
  transfers between devices with their start and end apart: 5, of which 3 were waited for; matrix products, arithmetic and copies ran while one was open for 1% of the time, Pallas kernels for 0%

commit v1 on v0

v1 whole, which is shorter than its diff:
```python
import functools
import math

import jax
import jax.numpy as jnp
from jax import lax
from jax.experimental import pallas as pl
from jax.experimental.pallas import tpu as pltpu
from jax.sharding import PartitionSpec as P

MESH = pl.DeviceIdType.MESH
GPS = 4
HD = 128
NZ, NY, NX = 4, 4, 2
SLOTS = NZ * NX
CHUNKS = NY
START = -1e30


def freshness(group_order):
    sections, groups = group_order.shape
    match = group_order[:, :, None] == jnp.arange(groups, dtype=jnp.int32)[None, None, :]
    turns = jnp.sum(
        jnp.arange(groups, dtype=jnp.int32)[None, :, None] * match.astype(jnp.int32), axis=1
    )
    times = (turns + jnp.arange(sections, dtype=jnp.int32)[:, None]).reshape(sections * groups)
    own = jnp.eye(sections * groups, dtype=jnp.bool_)
    return ((times[None, :] < times[:, None]) | own).astype(jnp.int32)


def kernel(
    fresh_ref, q_ref, k_ref, v_ref, sk_ref, sv_ref, out_ref,
    q_buf, kv_buf, acc, peak, part_out, part_in, lse_out, lse_in, done_buf,
    local_sem, q_send, q_recv, qf_send, qf_recv, kv_send, kv_recv, fwd_send, fwd_recv,
    part_send, part_recv, lse_send, lse_recv, done_send, done_recv,
):
    pipe, seq, tp = lax.axis_index("pipe"), lax.axis_index("seq"), lax.axis_index("tp")
    z, y, x = seq // (NY * NX), (seq // NX) % NY, seq % NX
    rows = q_ref.shape[0]
    block = NY * rows
    chunk_keys = 2 * SLOTS * rows
    scaling = math.log2(math.e) / math.sqrt(HD)
    sibling = {"tp": 1 - tp}
    across = {"pipe": 1 - pipe}

    def partner(dz, dy, dx):
        other = (((z + dz) % NZ) * NY + (y + dy) % NY) * NX + (x + dx) % NX
        return other, {"seq": other, "pipe": (pipe + dx) % 2}

    def offset(chunk, slot):
        dz, dx = slot % NZ, slot // NZ
        return dz, (dz + chunk) % NY, dx

    def remote(src, dst, send, recv, device):
        return pltpu.make_async_remote_copy(
            src_ref=src, dst_ref=dst, send_sem=send, recv_sem=recv,
            device_id=device, device_id_type=MESH,
        )

    def bytes_of(view, sem):
        pltpu.make_async_copy(view, view, sem).wait()

    barrier = pltpu.get_barrier_semaphore()

    def greet(index, _):
        _, device = partner(*offset(index // SLOTS, index % SLOTS))
        pl.semaphore_signal(barrier, inc=1, device_id=device, device_id_type=MESH)
        return 0

    lax.fori_loop(1, CHUNKS * SLOTS, greet, 0)
    pl.semaphore_signal(barrier, inc=1, device_id=sibling, device_id_type=MESH)
    pl.semaphore_signal(barrier, inc=1, device_id=across, device_id_type=MESH)
    pl.semaphore_wait(barrier, CHUNKS * SLOTS + 1)

    def head(ref, which):
        return ref.at[:, pl.ds(pl.multiple_of(which * HD, HD), HD)]

    def kv_refs():
        return ((k_ref, 0, 0), (sk_ref, 0, 1), (v_ref, 1, 0), (sv_ref, 1, 1))

    def send_queries(index, _):
        dz, dy, dx = offset(index // SLOTS, index % SLOTS)
        other, device = partner(dz, dy, dx)
        remote(head(q_ref, other), q_buf.at[0, dx, z, y], q_send, q_recv, device).start()
        return 0

    lax.fori_loop(1, CHUNKS * SLOTS, send_queries, 0)
    own_q = pltpu.make_async_copy(head(q_ref, seq), q_buf.at[0, 0, z, y], local_sem.at[0])
    own_q.start()

    def send_kv(index, _):
        chunk, slot = index // SLOTS, index % SLOTS
        other, device = partner(*offset(chunk, slot))
        for ref, kind, version in kv_refs():
            remote(
                head(ref, other), kv_buf.at[chunk, tp, slot, kind, version],
                kv_send.at[chunk], kv_recv.at[chunk], device,
            ).start()
        return 0

    lax.fori_loop(1, CHUNKS * SLOTS, send_kv, 0)
    own_kv = []
    for number, (ref, kind, version) in enumerate(kv_refs()):
        copy = pltpu.make_async_copy(
            head(ref, seq), kv_buf.at[0, tp, 0, kind, version], local_sem.at[1 + number]
        )
        copy.start()
        own_kv.append(copy)

    def clear(index, _):
        acc[index] = jnp.zeros(acc.shape[1:], jnp.float32)
        peak[index] = jnp.full(peak.shape[1:], START, jnp.float32)
        return 0

    lax.fori_loop(0, 4 * NZ, clear, 0)

    def others(ref):
        return ref.at[0, pl.ds(0, 7)]

    def forward_q():
        return remote(q_buf.at[0], q_buf.at[1], qf_send, qf_recv, across)

    def forward_kv(chunk):
        mine = kv_buf.at[chunk, tp]
        return remote(mine, mine, fwd_send.at[chunk], fwd_recv.at[chunk], sibling)

    def other_blocks(count_view, sem):
        bytes_of(count_view, sem)

    arrived = out_ref.at[:, pl.ds(0, (CHUNKS * SLOTS - 1) * HD)]
    bytes_of(arrived, q_recv)
    own_q.wait()
    forward_q().start()
    bytes_of(kv_buf.at[0, tp, pl.ds(1, SLOTS - 1)], kv_recv.at[0])
    for copy in own_kv:
        copy.wait()
    forward_kv(0).start()
    forward_kv(0).wait_recv()

    ones = jnp.ones((chunk_keys, HD), jnp.bfloat16)

    def chosen(chunk, kind, query_group):
        pieces = []
        for slot in range(SLOTS):
            key_group = ((pipe + slot // NZ) % 2) * GPS + (z + NZ - slot % NZ) % NZ
            fresh = fresh_ref[query_group, key_group] != 0
            for core in range(2):
                pieces.append(
                    jnp.where(
                        fresh,
                        kv_buf[chunk, core, slot, kind, 0],
                        kv_buf[chunk, core, slot, kind, 1],
                    )
                )
        return jnp.concatenate(pieces, axis=0)

    def attend(chunk, half, dx):
        first = (half * NX + dx) * NZ
        query_pipe = (pipe + dx + half) % 2

        def score(number):
            queries = q_buf[half, dx, number].reshape(block, HD)
            keys = chosen(chunk, 0, query_pipe * GPS + number)
            return lax.dot_general(
                queries, keys, (((1,), (1,)), ((), ())), preferred_element_type=jnp.float32
            )

        scores = score(0)
        for number in range(NZ):
            later = score(number + 1) if number + 1 < NZ else None
            values = chosen(chunk, 1, query_pipe * GPS + number)
            values = jnp.concatenate([values, ones], axis=1)
            before = peak[first + number, :, :1]
            now = jnp.maximum(before, jnp.max(scores, axis=1, keepdims=True) * scaling)
            weights = jnp.exp2(scores * scaling - now).astype(jnp.bfloat16)
            factor = jnp.exp2(before - now)
            acc[first + number] = acc[first + number] * factor + jnp.dot(
                weights, values, preferred_element_type=jnp.float32
            )
            peak[first + number] = jnp.broadcast_to(now, (block, HD))
            scores = later

    def finished(index):
        total = acc[index, :, HD : HD + 1]
        level = peak[index, :, :1] + jnp.log2(total)
        return acc[index, :, :HD] / total, level

    def exchange(dx):
        return (
            remote(part_out.at[dx], part_in.at[dx], part_send.at[dx], part_recv.at[dx], across),
            remote(lse_out.at[dx], lse_in.at[dx], lse_send.at[dx], lse_recv.at[dx], across),
        )

    def hand_over(dx):
        for number in range(NZ):
            mixed, level = finished((NX + dx) * NZ + number)
            part_out[dx, number] = mixed.astype(jnp.bfloat16)
            wide = jnp.concatenate(
                [
                    jnp.broadcast_to(level, (block, HD)),
                    jnp.zeros((lse_out.shape[3] - block, HD), jnp.float32),
                ],
                axis=0,
            )
            lse_out[dx, number] = jnp.transpose(wide)[:8]
        for copy in exchange(dx):
            copy.start()

    def give_back(dx):
        for copy in exchange(dx):
            copy.wait_recv()
        for number in range(NZ):
            mine, level = finished(dx * NZ + number)
            wide = jnp.concatenate(
                [lse_in[dx, number]] * (HD // 8), axis=0
            )
            other_level = jnp.transpose(wide)[:block, :1]
            top = jnp.maximum(level, other_level)
            share, other_share = jnp.exp2(level - top), jnp.exp2(other_level - top)
            both = 1.0 / (share + other_share)
            mixed = mine * (share * both) + part_in[dx, number].astype(jnp.float32) * (
                other_share * both
            )
            done_buf[dx, number] = mixed.astype(jnp.bfloat16).reshape(NY, rows, HD)

        def send_back(index, _):
            back_z, back_y = index // NY, index % NY
            other = (back_z * NY + back_y) * NX + (x + dx) % NX
            target = {"seq": other, "pipe": (pipe + dx) % 2}

            @pl.when(jnp.logical_or(other != seq, dx != 0))
            def _():
                remote(
                    done_buf.at[dx, back_z, back_y], head(out_ref, seq),
                    done_send, done_recv, target,
                ).start()

            return 0

        lax.fori_loop(0, NZ * NY, send_back, 0)

    def step(index, _):
        chunk, turn = index // 4, index % 4
        dx = turn % 2
        half = jnp.where(chunk == 0, turn // 2, 1 - turn // 2)

        @pl.when(index == 2)
        def _():
            forward_q().wait_recv()

        @pl.when(jnp.logical_and(turn == 0, chunk > 0))
        def _():
            forward_kv(chunk).wait_recv()

        @pl.when(jnp.logical_and(turn == 2, chunk < CHUNKS - 1))
        def _():
            bytes_of(kv_buf.at[chunk + 1, tp], kv_recv.at[chunk + 1])
            forward_kv(chunk + 1).start()

        attend(chunk, half, dx)

        @pl.when(jnp.logical_and(chunk == CHUNKS - 1, turn < 2))
        def _():
            hand_over(dx)

        @pl.when(jnp.logical_and(chunk == CHUNKS - 1, turn >= 2))
        def _():
            give_back(dx)

        return 0

    lax.fori_loop(0, 4 * CHUNKS, step, 0)

    own_out = pltpu.make_async_copy(done_buf.at[0, z, y], head(out_ref, seq), local_sem.at[5])
    own_out.start()
    own_out.wait()
    bytes_of(arrived, q_send)
    forward_q().wait_send()
    bytes_of(kv_buf.at[0, tp, pl.ds(1, SLOTS - 1)], kv_send.at[0])
    for chunk in range(1, CHUNKS):
        bytes_of(kv_buf.at[chunk, tp], kv_send.at[chunk])
    for chunk in range(CHUNKS):
        forward_kv(chunk).wait_send()
    for dx in range(NX):
        for copy in exchange(dx):
            copy.wait_send()
    bytes_of(arrived, done_send)
    bytes_of(arrived, done_recv)


def local(queries, keys, values, stale_keys, stale_values, group_order):
    rows, columns = queries.shape
    block = NY * rows
    dma = pltpu.SemaphoreType.DMA
    anywhere = pl.BlockSpec(memory_space=pl.ANY)
    return pl.pallas_call(
        kernel,
        out_shape=jax.ShapeDtypeStruct((rows, columns), jnp.bfloat16),
        in_specs=[pl.BlockSpec(memory_space=pltpu.SMEM)] + [anywhere] * 5,
        out_specs=anywhere,
        scratch_shapes=[
            pltpu.VMEM((2, NX, NZ, NY, rows, HD), jnp.bfloat16),
            pltpu.VMEM((CHUNKS, 2, SLOTS, 2, 2, rows, HD), jnp.bfloat16),
            pltpu.VMEM((2 * NX * NZ, block, 2 * HD), jnp.float32),
            pltpu.VMEM((2 * NX * NZ, block, HD), jnp.float32),
            pltpu.VMEM((NX, NZ, block, HD), jnp.bfloat16),
            pltpu.VMEM((NX, NZ, block, HD), jnp.bfloat16),
            pltpu.VMEM((NX, NZ, 8, 512), jnp.float32),
            pltpu.VMEM((NX, NZ, 8, 512), jnp.float32),
            pltpu.VMEM((NX, NZ, NY, rows, HD), jnp.bfloat16),
            dma((6,)), dma, dma, dma, dma,
            dma((CHUNKS,)), dma((CHUNKS,)), dma((CHUNKS,)), dma((CHUNKS,)),
            dma((NX,)), dma((NX,)), dma((NX,)), dma((NX,)), dma, dma,
        ],
        compiler_params=pltpu.CompilerParams(
            collective_id=0, has_side_effects=True, vmem_limit_bytes=60 * 2**20
        ),
    )(freshness(group_order), queries, keys, values, stale_keys, stale_values)


def solution(mesh):
    placed = P(("pipe", "seq", "tp"), None)
    return jax.shard_map(
        local, mesh=mesh, in_specs=(placed,) * 5 + (P(),), out_specs=placed, check_vma=False
    )
```

time: 520 us -> 143 us (0.28)
  matrix products: 148 us -> 0 us
  Pallas kernels: 0 us -> 138 us
  blocking collectives: 137 us -> 0 us
  waiting for transfers between devices: 109 us -> 0 us
  other arithmetic: 81.3 us -> 1.44 us
  local copies, waits for them, and re-layouts: 18.5 us -> 2.25 us
  between operations: 13.3 us -> 0.01 us
  starting transfers between devices: 6.2 us -> 0 us
    dot_general x64 -> x0, matrix products: 148 us -> none  [the longest x32 95.5 us: step_block(): lax.dot_general(query_blocks[number], chosen_keys, (((1,), (1,)), ((), ()...]
    pallas_call x0 -> x1, Pallas kernels: none -> 138 us  [local(): pl.pallas_call(kernel, out_shape=jax.ShapeDtypeStruct((rows, columns), jn...]
    all_to_all x5 -> x0, blocking collectives: 137 us -> none  [the longest x1 30 us: local(): lax.all_to_all(values, 'seq', split_axis=1, concat_axis=0, tiled=True)]
    all_gather x4 -> x0, waiting for transfers between devices: 87.5 us -> none  [the longest x1 44.6 us: local(): lax.all_gather(old_values, ('pipe', 'tp'), axis=0, tiled=True)]
    or x8 -> x0, other arithmetic: 42.2 us -> none  [step_block(): (key_time < query_times[number]) | (key_group == query_groups[number])]
    reduce_sum x42 -> x1, other arithmetic: 36.4 us -> 0.76 us  [freshness(): jnp.sum(jnp.arange(groups, dtype=jnp.int32)[None, :, None] * match.astype...]
    all_to_all x1 -> x0, waiting for transfers between devices: 21.5 us -> none  [local(): lax.all_to_all(queries, 'seq', split_axis=1, concat_axis=0, tiled=True)]
    while x48 -> x0, local copies, waits for them, and re-layouts: 7.31 us -> none
  transfers between devices with their start and end apart: 5 -> 0, of which waited for: 3 -> 0; matrix products, arithmetic and copies ran while one was open for 1% -> 0% of each run, Pallas kernels for 0% -> 0%
where the time goes in v1:
time: 143 us; the launch traced here: 142 us
  Pallas kernels  138 us (97%)
  local copies, waits for them, and re-layouts  2.25 us (2%)
  other arithmetic  1.44 us (1%)
    pallas_call x1, Pallas kernels, local(): pl.pallas_call(kernel, out_shape=jax.ShapeDtypeStruct((rows, columns), jn...  138 us

profile of v1, /device:TPU:96, one launch (start us, length us, event | category | flops | bytes accessed | tf_op | source)
XLA Modules:
  0.0 141.7 jit_solution(2252924926919562253)
XLA Ops:
  0.0 0.8 select_reduce_fusion
  0.8 0.1 add.21
  0.9 0.7 fusion.1.fresh_ref
  1.5 138.0 %shard_map.64 = bf16[112,4096]{1,0:T(8,128)(2,1)} custom-call(s32[8,8]{1,0:T(8,128)} %fusion.1.fresh_ref, bf16[112,4096]{1,0:T(8,128)(2,1)} %q_ref.1, bf16[112,4096]{1,0:T(8,128)(2,1)} %k_ref.1, bf16[112,4096]{1,0:T(8,128)(2,1)} %v_ref.1, bf16[112,4096]{1,0:T(8,128)(2,1)} %sk_ref.1, bf16[112,4096]{1,0:T(8,128)(2,1)} %sv_ref.1), custom_call_target="tpu_custom_call" | custom-call | tf_op jit(solution)/shard_map/pallas_call | solution.py:296
  139.5 2.2 %copy.8 = bf16[112,4096]{1,0:T(8,128)(2,1)} copy(bf16[112,4096]{1,0:T(8,128)(2,1)} %shard_map.64) | data formatting | bytes 1835008
  (1 shorter events, 0.0 us)

commit v2 on v1

--- a/solution.py
+++ b/solution.py
@@ -17,20 +17,30 @@
 START = -1e30
 
 
-def freshness(group_order):
-    sections, groups = group_order.shape
-    match = group_order[:, :, None] == jnp.arange(groups, dtype=jnp.int32)[None, None, :]
-    turns = jnp.sum(
-        jnp.arange(groups, dtype=jnp.int32)[None, :, None] * match.astype(jnp.int32), axis=1
-    )
-    times = (turns + jnp.arange(sections, dtype=jnp.int32)[:, None]).reshape(sections * groups)
-    own = jnp.eye(sections * groups, dtype=jnp.bool_)
-    return ((times[None, :] < times[:, None]) | own).astype(jnp.int32)
+STEPS = (
+    ((0, 0, 0), (0, 0, 1), (1, 0, 0), (3, 0, 0), (0, 1, 0), (0, 3, 0), (1, 1, 1), (3, 3, 0)),
+    ((0, 2, 0), (3, 1, 1), (2, 0, 1), (3, 1, 0), (2, 3, 0), (1, 3, 1), (0, 1, 1), (1, 3, 0)),
+    ((2, 0, 0), (0, 3, 1), (3, 2, 0), (0, 2, 1), (2, 1, 1), (1, 0, 1), (2, 2, 0), (2, 2, 1)),
+    ((3, 3, 1), (2, 1, 0), (1, 1, 0), (2, 3, 1), (1, 2, 0), (3, 2, 1), (3, 0, 1), (1, 2, 1)),
+)
+ORDER = (
+    (0, 0, 0), (0, 1, 0), (1, 0, 0), (0, 0, 1), (0, 1, 1), (1, 1, 0), (1, 0, 1), (1, 1, 1),
+    (1, 0, 2), (1, 1, 2), (1, 0, 3), (1, 1, 3), (0, 0, 2), (0, 0, 3), (0, 1, 2), (0, 1, 3),
+)
+
+
+def lookup(index, table):
+    found = table[0]
+    for at in range(1, len(table)):
+        if table[at] != table[at - 1]:
+            found = jnp.where(index >= at, table[at], found)
+    return found
 
 
 def kernel(
-    fresh_ref, q_ref, k_ref, v_ref, sk_ref, sv_ref, out_ref,
+    order_ref, q_ref, k_ref, v_ref, sk_ref, sv_ref, out_ref,
     q_buf, kv_buf, acc, peak, part_out, part_in, lse_out, lse_in, done_buf,
+    time_ref, group_ref,
     local_sem, q_send, q_recv, qf_send, qf_recv, kv_send, kv_recv, fwd_send, fwd_recv,
     part_send, part_recv, lse_send, lse_recv, done_send, done_recv,
 ):
@@ -47,10 +57,6 @@
         other = (((z + dz) % NZ) * NY + (y + dy) % NY) * NX + (x + dx) % NX
         return other, {"seq": other, "pipe": (pipe + dx) % 2}
 
-    def offset(chunk, slot):
-        dz, dx = slot % NZ, slot // NZ
-        return dz, (dz + chunk) % NY, dx
-
     def remote(src, dst, send, recv, device):
         return pltpu.make_async_remote_copy(
             src_ref=src, dst_ref=dst, send_sem=send, recv_sem=recv,
@@ -63,7 +69,7 @@
     barrier = pltpu.get_barrier_semaphore()
 
     def greet(index, _):
-        _, device = partner(*offset(index // SLOTS, index % SLOTS))
+        _, device = partner(index // (NY * NX), (index // NX) % NY, index % NX)
         pl.semaphore_signal(barrier, inc=1, device_id=device, device_id_type=MESH)
         return 0
 
@@ -78,27 +84,37 @@
     def kv_refs():
         return ((k_ref, 0, 0), (sk_ref, 0, 1), (v_ref, 1, 0), (sv_ref, 1, 1))
 
+    def send_kv(chunk):
+        for slot, step in enumerate(STEPS[chunk]):
+            if step == (0, 0, 0):
+                continue
+            other, device = partner(*step)
+            for ref, kind, version in kv_refs():
+                remote(
+                    head(ref, other), kv_buf.at[chunk, tp, slot, kind, version],
+                    kv_send.at[chunk], kv_recv.at[chunk], device,
+                ).start()
+
     def send_queries(index, _):
-        dz, dy, dx = offset(index // SLOTS, index % SLOTS)
-        other, device = partner(dz, dy, dx)
-        remote(head(q_ref, other), q_buf.at[0, dx, z, y], q_send, q_recv, device).start()
+        dx, step = index // (NZ * NY), index % (NZ * NY)
+        dz = step % NZ
+        other, device = partner(dz, (dz + step // NZ) % NY, dx)
+        remote(
+            head(q_ref, other), q_buf.at[0, dx, z, y], q_send.at[dx], q_recv.at[dx], device
+        ).start()
         return 0
 
-    lax.fori_loop(1, CHUNKS * SLOTS, send_queries, 0)
-    own_q = pltpu.make_async_copy(head(q_ref, seq), q_buf.at[0, 0, z, y], local_sem.at[0])
-    own_q.start()
-
-    def send_kv(index, _):
-        chunk, slot = index // SLOTS, index % SLOTS
-        other, device = partner(*offset(chunk, slot))
-        for ref, kind, version in kv_refs():
-            remote(
-                head(ref, other), kv_buf.at[chunk, tp, slot, kind, version],
-                kv_send.at[chunk], kv_recv.at[chunk], device,
-            ).start()
-        return 0
-
-    lax.fori_loop(1, CHUNKS * SLOTS, send_kv, 0)
+    for chunk in range(CHUNKS):
+        for slot, (dz, _, dx) in enumerate(STEPS[chunk]):
+            group_ref[chunk * SLOTS + slot] = ((pipe + dx) % 2) * GPS + (z + NZ - dz) % NZ
+    for section in range(2):
+        for group in range(GPS):
+            when = section
+            for turn in range(GPS):
+                when = when + jnp.where(order_ref[section, turn] == group, turn, 0)
+            time_ref[section * GPS + group] = when
+
+    send_kv(0)
     own_kv = []
     for number, (ref, kind, version) in enumerate(kv_refs()):
         copy = pltpu.make_async_copy(
@@ -106,6 +122,9 @@
         )
         copy.start()
         own_kv.append(copy)
+    own_q = pltpu.make_async_copy(head(q_ref, seq), q_buf.at[0, 0, z, y], local_sem.at[0])
+    own_q.start()
+    lax.fori_loop(1, NZ * NY, send_queries, 0)
 
     def clear(index, _):
         acc[index] = jnp.zeros(acc.shape[1:], jnp.float32)
@@ -114,27 +133,25 @@
 
     lax.fori_loop(0, 4 * NZ, clear, 0)
 
-    def others(ref):
-        return ref.at[0, pl.ds(0, 7)]
-
-    def forward_q():
-        return remote(q_buf.at[0], q_buf.at[1], qf_send, qf_recv, across)
+    def forward_q(dx):
+        return remote(q_buf.at[0, dx], q_buf.at[1, dx], qf_send.at[dx], qf_recv.at[dx], across)
 
     def forward_kv(chunk):
         mine = kv_buf.at[chunk, tp]
         return remote(mine, mine, fwd_send.at[chunk], fwd_recv.at[chunk], sibling)
 
-    def other_blocks(count_view, sem):
-        bytes_of(count_view, sem)
-
-    arrived = out_ref.at[:, pl.ds(0, (CHUNKS * SLOTS - 1) * HD)]
-    bytes_of(arrived, q_recv)
-    own_q.wait()
-    forward_q().start()
+    def blocks(count):
+        return out_ref.at[:, pl.ds(0, count * HD)]
+
     bytes_of(kv_buf.at[0, tp, pl.ds(1, SLOTS - 1)], kv_recv.at[0])
     for copy in own_kv:
         copy.wait()
     forward_kv(0).start()
+    lax.fori_loop(NZ * NY, CHUNKS * SLOTS, send_queries, 0)
+    own_q.wait()
+    bytes_of(blocks(NZ * NY - 1), q_recv.at[0])
+    forward_q(0).start()
+    send_kv(1)
     forward_kv(0).wait_recv()
 
     ones = jnp.ones((chunk_keys, HD), jnp.bfloat16)
@@ -142,8 +159,10 @@
     def chosen(chunk, kind, query_group):
         pieces = []
         for slot in range(SLOTS):
-            key_group = ((pipe + slot // NZ) % 2) * GPS + (z + NZ - slot % NZ) % NZ
-            fresh = fresh_ref[query_group, key_group] != 0
+            key_group = group_ref[chunk * SLOTS + slot]
+            fresh = jnp.logical_or(
+                time_ref[key_group] < time_ref[query_group], key_group == query_group
+            )
             for core in range(2):
                 pieces.append(
                     jnp.where(
@@ -211,9 +230,7 @@
             copy.wait_recv()
         for number in range(NZ):
             mine, level = finished(dx * NZ + number)
-            wide = jnp.concatenate(
-                [lse_in[dx, number]] * (HD // 8), axis=0
-            )
+            wide = jnp.concatenate([lse_in[dx, number]] * (HD // 8), axis=0)
             other_level = jnp.transpose(wide)[:block, :1]
             top = jnp.maximum(level, other_level)
             share, other_share = jnp.exp2(level - top), jnp.exp2(other_level - top)
@@ -223,47 +240,61 @@
             )
             done_buf[dx, number] = mixed.astype(jnp.bfloat16).reshape(NY, rows, HD)
 
-        def send_back(index, _):
-            back_z, back_y = index // NY, index % NY
-            other = (back_z * NY + back_y) * NX + (x + dx) % NX
-            target = {"seq": other, "pipe": (pipe + dx) % 2}
-
-            @pl.when(jnp.logical_or(other != seq, dx != 0))
+            def send_back(back_y, _):
+                other = (number * NY + back_y) * NX + (x + dx) % NX
+                target = {"seq": other, "pipe": (pipe + dx) % 2}
+
+                @pl.when(jnp.logical_or(other != seq, dx != 0))
+                def _():
+                    remote(
+                        done_buf.at[dx, number, back_y], head(out_ref, seq),
+                        done_send, done_recv, target,
+                    ).start()
+
+                return 0
+
+            lax.fori_loop(0, NY, send_back, 0)
+
+    def step(index, _):
+        half, dx, chunk = (lookup(index, [entry[at] for entry in ORDER]) for at in range(3))
+
+        @pl.when(index == 1)
+        def _():
+            bytes_of(blocks(NZ * NY), q_recv.at[1])
+            forward_q(1).start()
+
+        @pl.when(jnp.logical_or(index == 2, index == 5))
+        def _():
+            forward_q(dx).wait_recv()
+
+        for at, number in ((3, 1), (6, 2), (8, 3)):
+
+            @pl.when(index == at)
             def _():
-                remote(
-                    done_buf.at[dx, back_z, back_y], head(out_ref, seq),
-                    done_send, done_recv, target,
-                ).start()
-
-            return 0
-
-        lax.fori_loop(0, NZ * NY, send_back, 0)
-
-    def step(index, _):
-        chunk, turn = index // 4, index % 4
-        dx = turn % 2
-        half = jnp.where(chunk == 0, turn // 2, 1 - turn // 2)
+                bytes_of(kv_buf.at[number, tp], kv_recv.at[number])
+                forward_kv(number).start()
+
+        for at, number in ((3, 1), (8, 2), (10, 3)):
+
+            @pl.when(index == at)
+            def _():
+                forward_kv(number).wait_recv()
 
         @pl.when(index == 2)
         def _():
-            forward_q().wait_recv()
-
-        @pl.when(jnp.logical_and(turn == 0, chunk > 0))
-        def _():
-            forward_kv(chunk).wait_recv()
-
-        @pl.when(jnp.logical_and(turn == 2, chunk < CHUNKS - 1))
-        def _():
-            bytes_of(kv_buf.at[chunk + 1, tp], kv_recv.at[chunk + 1])
-            forward_kv(chunk + 1).start()
+            send_kv(2)
+
+        @pl.when(index == 4)
+        def _():
+            send_kv(3)
 
         attend(chunk, half, dx)
 
-        @pl.when(jnp.logical_and(chunk == CHUNKS - 1, turn < 2))
+        @pl.when(jnp.logical_or(index == 10, index == 11))
         def _():
             hand_over(dx)
 
-        @pl.when(jnp.logical_and(chunk == CHUNKS - 1, turn >= 2))
+        @pl.when(jnp.logical_or(index == 13, index == 15))
         def _():
             give_back(dx)
 
@@ -274,8 +305,9 @@
     own_out = pltpu.make_async_copy(done_buf.at[0, z, y], head(out_ref, seq), local_sem.at[5])
     own_out.start()
     own_out.wait()
-    bytes_of(arrived, q_send)
-    forward_q().wait_send()
+    for dx in range(NX):
+        bytes_of(blocks(NZ * NY - 1 + dx), q_send.at[dx])
+        forward_q(dx).wait_send()
     bytes_of(kv_buf.at[0, tp, pl.ds(1, SLOTS - 1)], kv_send.at[0])
     for chunk in range(1, CHUNKS):
         bytes_of(kv_buf.at[chunk, tp], kv_send.at[chunk])
@@ -284,8 +316,8 @@
     for dx in range(NX):
         for copy in exchange(dx):
             copy.wait_send()
-    bytes_of(arrived, done_send)
-    bytes_of(arrived, done_recv)
+    bytes_of(blocks(CHUNKS * SLOTS - 1), done_send)
+    bytes_of(blocks(CHUNKS * SLOTS - 1), done_recv)
 
 
 def local(queries, keys, values, stale_keys, stale_values, group_order):
@@ -308,14 +340,16 @@
             pltpu.VMEM((NX, NZ, 8, 512), jnp.float32),
             pltpu.VMEM((NX, NZ, 8, 512), jnp.float32),
             pltpu.VMEM((NX, NZ, NY, rows, HD), jnp.bfloat16),
-            dma((6,)), dma, dma, dma, dma,
+            pltpu.SMEM((2 * GPS,), jnp.int32),
+            pltpu.SMEM((CHUNKS * SLOTS,), jnp.int32),
+            dma((6,)), dma((NX,)), dma((NX,)), dma((NX,)), dma((NX,)),
             dma((CHUNKS,)), dma((CHUNKS,)), dma((CHUNKS,)), dma((CHUNKS,)),
             dma((NX,)), dma((NX,)), dma((NX,)), dma((NX,)), dma, dma,
         ],
         compiler_params=pltpu.CompilerParams(
             collective_id=0, has_side_effects=True, vmem_limit_bytes=60 * 2**20
         ),
-    )(freshness(group_order), queries, keys, values, stale_keys, stale_values)
+    )(group_order, queries, keys, values, stale_keys, stale_values)
 
 
 def solution(mesh):

time: 143 us -> 127 us (0.89)
  Pallas kernels: 138 us -> 123 us
  other arithmetic: 1.44 us -> 0 us
    pallas_call x1, Pallas kernels: 138 us -> 123 us  [local(): pl.pallas_call(kernel, out_shape=jax.ShapeDtypeStruct((rows, columns), jn...]
where the time goes in v2:
time: 127 us; the launch traced here: 125 us
  Pallas kernels  123 us (97%)
  local copies, waits for them, and re-layouts  2.17 us (2%)
    pallas_call x1, Pallas kernels, local(): pl.pallas_call(kernel, out_shape=jax.ShapeDtypeStruct((rows, columns), jn...  123 us

profile of v2, /device:TPU:96, one launch (start us, length us, event | category | flops | bytes accessed | tf_op | source)
XLA Modules:
  0.0 125.0 jit_solution(4610188585398093043)
XLA Ops:
  0.0 122.9 %shard_map.64 = bf16[112,4096]{1,0:T(8,128)(2,1)} custom-call(s32[2,4]{1,0:T(2,128)} %order_ref.1, bf16[112,4096]{1,0:T(8,128)(2,1)} %q_ref.1, bf16[112,4096]{1,0:T(8,128)(2,1)} %k_ref.1, bf16[112,4096]{1,0:T(8,128)(2,1)} %v_ref.1, bf16[112,4096]{1,0:T(8,128)(2,1)} %sk_ref.1, bf16[112,4096]{1,0:T(8,128)(2,1)} %sv_ref.1), custom_call_target="tpu_custom_call" | custom-call | tf_op jit(solution)/shard_map/pallas_call | solution.py:328
  122.9 2.2 %copy.8 = bf16[112,4096]{1,0:T(8,128)(2,1)} copy(bf16[112,4096]{1,0:T(8,128)(2,1)} %shard_map.64) | data formatting | bytes 1835008

commit v3 on v2

--- a/solution.py
+++ b/solution.py
@@ -24,7 +24,7 @@
     ((3, 3, 1), (2, 1, 0), (1, 1, 0), (2, 3, 1), (1, 2, 0), (3, 2, 1), (3, 0, 1), (1, 2, 1)),
 )
 ORDER = (
-    (0, 0, 0), (0, 1, 0), (1, 0, 0), (0, 0, 1), (0, 1, 1), (1, 1, 0), (1, 0, 1), (1, 1, 1),
+    (0, 0, 0), (0, 1, 0), (1, 0, 0), (1, 1, 0), (0, 0, 1), (0, 1, 1), (1, 0, 1), (1, 1, 1),
     (1, 0, 2), (1, 1, 2), (1, 0, 3), (1, 1, 3), (0, 0, 2), (0, 0, 3), (0, 1, 2), (0, 1, 3),
 )
 
@@ -124,7 +124,7 @@
         own_kv.append(copy)
     own_q = pltpu.make_async_copy(head(q_ref, seq), q_buf.at[0, 0, z, y], local_sem.at[0])
     own_q.start()
-    lax.fori_loop(1, NZ * NY, send_queries, 0)
+    lax.fori_loop(1, CHUNKS * SLOTS, send_queries, 0)
 
     def clear(index, _):
         acc[index] = jnp.zeros(acc.shape[1:], jnp.float32)
@@ -147,11 +147,10 @@
     for copy in own_kv:
         copy.wait()
     forward_kv(0).start()
-    lax.fori_loop(NZ * NY, CHUNKS * SLOTS, send_queries, 0)
+    send_kv(1)
     own_q.wait()
     bytes_of(blocks(NZ * NY - 1), q_recv.at[0])
     forward_q(0).start()
-    send_kv(1)
     forward_kv(0).wait_recv()
 
     ones = jnp.ones((chunk_keys, HD), jnp.bfloat16)
@@ -258,35 +257,33 @@
     def step(index, _):
         half, dx, chunk = (lookup(index, [entry[at] for entry in ORDER]) for at in range(3))
 
+        for at, number in ((1, 2), (3, 3)):
+
+            @pl.when(index == at)
+            def _():
+                send_kv(number)
+
         @pl.when(index == 1)
         def _():
             bytes_of(blocks(NZ * NY), q_recv.at[1])
             forward_q(1).start()
 
-        @pl.when(jnp.logical_or(index == 2, index == 5))
+        @pl.when(jnp.logical_or(index == 2, index == 3))
         def _():
             forward_q(dx).wait_recv()
 
-        for at, number in ((3, 1), (6, 2), (8, 3)):
+        for at, number in ((3, 1), (7, 2), (9, 3)):
 
             @pl.when(index == at)
             def _():
                 bytes_of(kv_buf.at[number, tp], kv_recv.at[number])
                 forward_kv(number).start()
 
-        for at, number in ((3, 1), (8, 2), (10, 3)):
+        for at, number in ((4, 1), (8, 2), (10, 3)):
 
             @pl.when(index == at)
             def _():
                 forward_kv(number).wait_recv()
-
-        @pl.when(index == 2)
-        def _():
-            send_kv(2)
-
-        @pl.when(index == 4)
-        def _():
-            send_kv(3)
 
         attend(chunk, half, dx)
 

time: 127 us -> 123 us (0.969); the launches traced: 125 us -> 123 us
  Pallas kernels: 123 us -> 121 us
    pallas_call x1, Pallas kernels: 123 us -> 121 us  [local(): pl.pallas_call(kernel, out_shape=jax.ShapeDtypeStruct((rows, columns), jn...]
where the time goes in v3:
time: 123 us
  Pallas kernels  121 us (98%)
  local copies, waits for them, and re-layouts  2.17 us (2%)
    pallas_call x1, Pallas kernels, local(): pl.pallas_call(kernel, out_shape=jax.ShapeDtypeStruct((rows, columns), jn...  121 us

profile of v3, /device:TPU:96, one launch (start us, length us, event | category | flops | bytes accessed | tf_op | source)
XLA Modules:
  0.0 123.1 jit_solution(6290571484319671274)
XLA Ops:
  0.0 120.9 %shard_map.64 = bf16[112,4096]{1,0:T(8,128)(2,1)} custom-call(s32[2,4]{1,0:T(2,128)} %order_ref.1, bf16[112,4096]{1,0:T(8,128)(2,1)} %q_ref.1, bf16[112,4096]{1,0:T(8,128)(2,1)} %k_ref.1, bf16[112,4096]{1,0:T(8,128)(2,1)} %v_ref.1, bf16[112,4096]{1,0:T(8,128)(2,1)} %sk_ref.1, bf16[112,4096]{1,0:T(8,128)(2,1)} %sv_ref.1), custom_call_target="tpu_custom_call" | custom-call | tf_op jit(solution)/shard_map/pallas_call | solution.py:325
  120.9 2.2 %copy.8 = bf16[112,4096]{1,0:T(8,128)(2,1)} copy(bf16[112,4096]{1,0:T(8,128)(2,1)} %shard_map.64) | data formatting | bytes 1835008

commit v4 on v3

--- a/solution.py
+++ b/solution.py
@@ -76,6 +76,16 @@
     lax.fori_loop(1, CHUNKS * SLOTS, greet, 0)
     pl.semaphore_signal(barrier, inc=1, device_id=sibling, device_id_type=MESH)
     pl.semaphore_signal(barrier, inc=1, device_id=across, device_id_type=MESH)
+    for chunk in range(CHUNKS):
+        for slot, (dz, _, dx) in enumerate(STEPS[chunk]):
+            group_ref[chunk * SLOTS + slot] = ((pipe + dx) % 2) * GPS + (z + NZ - dz) % NZ
+    for section in range(2):
+        for group in range(GPS):
+            when = section
+            for turn in range(GPS):
+                when = when + jnp.where(order_ref[section, turn] == group, turn, 0)
+            time_ref[section * GPS + group] = when
+
     pl.semaphore_wait(barrier, CHUNKS * SLOTS + 1)
 
     def head(ref, which):
@@ -104,17 +114,10 @@
         ).start()
         return 0
 
-    for chunk in range(CHUNKS):
-        for slot, (dz, _, dx) in enumerate(STEPS[chunk]):
-            group_ref[chunk * SLOTS + slot] = ((pipe + dx) % 2) * GPS + (z + NZ - dz) % NZ
-    for section in range(2):
-        for group in range(GPS):
-            when = section
-            for turn in range(GPS):
-                when = when + jnp.where(order_ref[section, turn] == group, turn, 0)
-            time_ref[section * GPS + group] = when
-
+    lax.fori_loop(1, CHUNKS * SLOTS, send_queries, 0)
     send_kv(0)
+    own_q = pltpu.make_async_copy(head(q_ref, seq), q_buf.at[0, 0, z, y], local_sem.at[0])
+    own_q.start()
     own_kv = []
     for number, (ref, kind, version) in enumerate(kv_refs()):
         copy = pltpu.make_async_copy(
@@ -122,9 +125,6 @@
         )
         copy.start()
         own_kv.append(copy)
-    own_q = pltpu.make_async_copy(head(q_ref, seq), q_buf.at[0, 0, z, y], local_sem.at[0])
-    own_q.start()
-    lax.fori_loop(1, CHUNKS * SLOTS, send_queries, 0)
 
     def clear(index, _):
         acc[index] = jnp.zeros(acc.shape[1:], jnp.float32)
@@ -143,14 +143,16 @@
     def blocks(count):
         return out_ref.at[:, pl.ds(0, count * HD)]
 
+    own_q.wait()
+    for dx in range(NX):
+        bytes_of(blocks(NZ * NY - 1 + dx), q_recv.at[dx])
+        forward_q(dx).start()
     bytes_of(kv_buf.at[0, tp, pl.ds(1, SLOTS - 1)], kv_recv.at[0])
     for copy in own_kv:
         copy.wait()
     forward_kv(0).start()
     send_kv(1)
-    own_q.wait()
-    bytes_of(blocks(NZ * NY - 1), q_recv.at[0])
-    forward_q(0).start()
+    send_kv(2)
     forward_kv(0).wait_recv()
 
     ones = jnp.ones((chunk_keys, HD), jnp.bfloat16)
@@ -210,27 +212,31 @@
         )
 
     def hand_over(dx):
+        lane = lax.broadcasted_iota(jnp.int32, (block, HD), 1)
+        levels = jnp.zeros((block, HD), jnp.float32)
         for number in range(NZ):
             mixed, level = finished((NX + dx) * NZ + number)
             part_out[dx, number] = mixed.astype(jnp.bfloat16)
-            wide = jnp.concatenate(
-                [
-                    jnp.broadcast_to(level, (block, HD)),
-                    jnp.zeros((lse_out.shape[3] - block, HD), jnp.float32),
-                ],
-                axis=0,
-            )
-            lse_out[dx, number] = jnp.transpose(wide)[:8]
-        for copy in exchange(dx):
-            copy.start()
+            remote(
+                part_out.at[dx, number], part_in.at[dx, number],
+                part_send.at[dx], part_recv.at[dx], across,
+            ).start()
+            levels = jnp.where(lane == number, level, levels)
+        wide = jnp.concatenate(
+            [levels, jnp.zeros((lse_out.shape[2] - block, HD), jnp.float32)], axis=0
+        )
+        lse_out[dx] = jnp.transpose(wide)[:8]
+        remote(
+            lse_out.at[dx], lse_in.at[dx], lse_send.at[dx], lse_recv.at[dx], across
+        ).start()
 
     def give_back(dx):
         for copy in exchange(dx):
             copy.wait_recv()
+        other_levels = jnp.transpose(jnp.concatenate([lse_in[dx]] * (HD // 8), axis=0))[:block]
         for number in range(NZ):
             mine, level = finished(dx * NZ + number)
-            wide = jnp.concatenate([lse_in[dx, number]] * (HD // 8), axis=0)
-            other_level = jnp.transpose(wide)[:block, :1]
+            other_level = other_levels[:, number : number + 1]
             top = jnp.maximum(level, other_level)
             share, other_share = jnp.exp2(level - top), jnp.exp2(other_level - top)
             both = 1.0 / (share + other_share)
@@ -257,16 +263,11 @@
     def step(index, _):
         half, dx, chunk = (lookup(index, [entry[at] for entry in ORDER]) for at in range(3))
 
-        for at, number in ((1, 2), (3, 3)):
+        for at, number in ((5, 3),):
 
             @pl.when(index == at)
             def _():
                 send_kv(number)
-
-        @pl.when(index == 1)
-        def _():
-            bytes_of(blocks(NZ * NY), q_recv.at[1])
-            forward_q(1).start()
 
         @pl.when(jnp.logical_or(index == 2, index == 3))
         def _():
@@ -334,8 +335,8 @@
             pltpu.VMEM((2 * NX * NZ, block, HD), jnp.float32),
             pltpu.VMEM((NX, NZ, block, HD), jnp.bfloat16),
             pltpu.VMEM((NX, NZ, block, HD), jnp.bfloat16),
-            pltpu.VMEM((NX, NZ, 8, 512), jnp.float32),
-            pltpu.VMEM((NX, NZ, 8, 512), jnp.float32),
+            pltpu.VMEM((NX, 8, 512), jnp.float32),
+            pltpu.VMEM((NX, 8, 512), jnp.float32),
             pltpu.VMEM((NX, NZ, NY, rows, HD), jnp.bfloat16),
             pltpu.SMEM((2 * GPS,), jnp.int32),
             pltpu.SMEM((CHUNKS * SLOTS,), jnp.int32),

time: 123 us -> 121 us (0.984)
  Pallas kernels: 121 us -> 119 us
    pallas_call x1, Pallas kernels: 121 us -> 119 us  [local(): pl.pallas_call(kernel, out_shape=jax.ShapeDtypeStruct((rows, columns), jn...]
where the time goes in v4:
time: 121 us
  Pallas kernels  119 us (98%)
  local copies, waits for them, and re-layouts  2.17 us (2%)
    pallas_call x1, Pallas kernels, local(): pl.pallas_call(kernel, out_shape=jax.ShapeDtypeStruct((rows, columns), jn...  119 us

profile of v4, /device:TPU:96, one launch (start us, length us, event | category | flops | bytes accessed | tf_op | source)
XLA Modules:
  0.0 120.9 jit_solution(6099014017758240426)
XLA Ops:
  0.0 118.8 %shard_map.64 = bf16[112,4096]{1,0:T(8,128)(2,1)} custom-call(s32[2,4]{1,0:T(2,128)} %order_ref.1, bf16[112,4096]{1,0:T(8,128)(2,1)} %q_ref.1, bf16[112,4096]{1,0:T(8,128)(2,1)} %k_ref.1, bf16[112,4096]{1,0:T(8,128)(2,1)} %v_ref.1, bf16[112,4096]{1,0:T(8,128)(2,1)} %sk_ref.1, bf16[112,4096]{1,0:T(8,128)(2,1)} %sv_ref.1), custom_call_target="tpu_custom_call" | custom-call | tf_op jit(solution)/shard_map/pallas_call | solution.py:326
  118.8 2.2 %copy.8 = bf16[112,4096]{1,0:T(8,128)(2,1)} copy(bf16[112,4096]{1,0:T(8,128)(2,1)} %shard_map.64) | data formatting | bytes 1835008

commit v5 on v4

--- a/solution.py
+++ b/solution.py
@@ -263,7 +263,7 @@
     def step(index, _):
         half, dx, chunk = (lookup(index, [entry[at] for entry in ORDER]) for at in range(3))
 
-        for at, number in ((5, 3),):
+        for at, number in ((6, 3),):
 
             @pl.when(index == at)
             def _():

time: 121 us -> 125 us (1.033)
  Pallas kernels: 119 us -> 123 us
    pallas_call x1, Pallas kernels: 119 us -> 123 us  [local(): pl.pallas_call(kernel, out_shape=jax.ShapeDtypeStruct((rows, columns), jn...]
where the time goes in v5:
time: 125 us
  Pallas kernels  123 us (98%)
  local copies, waits for them, and re-layouts  2.17 us (2%)
    pallas_call x1, Pallas kernels, local(): pl.pallas_call(kernel, out_shape=jax.ShapeDtypeStruct((rows, columns), jn...  123 us

profile of v5, /device:TPU:96, one launch (start us, length us, event | category | flops | bytes accessed | tf_op | source)
XLA Modules:
  0.0 125.2 jit_solution(883680152642873825)
XLA Ops:
  0.0 123.1 %shard_map.64 = bf16[112,4096]{1,0:T(8,128)(2,1)} custom-call(s32[2,4]{1,0:T(2,128)} %order_ref.1, bf16[112,4096]{1,0:T(8,128)(2,1)} %q_ref.1, bf16[112,4096]{1,0:T(8,128)(2,1)} %k_ref.1, bf16[112,4096]{1,0:T(8,128)(2,1)} %v_ref.1, bf16[112,4096]{1,0:T(8,128)(2,1)} %sk_ref.1, bf16[112,4096]{1,0:T(8,128)(2,1)} %sv_ref.1), custom_call_target="tpu_custom_call" | custom-call | tf_op jit(solution)/shard_map/pallas_call | solution.py:326
  123.1 2.2 %copy.8 = bf16[112,4096]{1,0:T(8,128)(2,1)} copy(bf16[112,4096]{1,0:T(8,128)(2,1)} %shard_map.64) | data formatting | bytes 1835008
